TPU v7x, 512 devices: a whole 4x8x8 slice. The times are simulated.
512 devices in a mesh: band: 32 (over y_lo, z), slab: 16 (over y_hi, x, core).
Axes of the slice: x: 4, y: 8 (y_hi: 2, y_lo: 4; y = y_hi * 4 + y_lo), z: 8, core: 2. Of those that a mesh axis runs over, the one named last changes fastest.
Arguments:
- orbitals: float32 [64, 160, 160, 128], P('band', 'slab'), may hold values from -4 to 4
- plan: int32 [32, 2, 2], replicated, may hold values from 0 to 3, all different within a row
Outputs:
- exchange: float32 [64, 160, 160, 128], P('band', 'slab')
Inputs may be any that keep to these rules, and one draw needn't show every extreme that they name: Code 2 * a + c in plan[e, 0] pairs band a of block e with band c of block e - 1 (mod 32); in plan[e, 1] with band c of block e + 1. The 2 codes of one block and side are distinct.
All inputs are finite; a program needn't handle non-finite values.
Results may differ from a plain program's by a relative error of at most 0.0004.
Values sent between devices are 32-bit elements; how exact they have to be, the bound alone decides.
A program may use at most 64 MiB of HBM per device.

v0:
```python
import math

import jax
import jax.numpy as jnp
from jax import lax
from jax.sharding import PartitionSpec as P

NX = 128
NY = 160
NZ = 160


MU_SQUARED = 0.0025
MIXING = 0.25
HIGHEST = lax.Precision.HIGHEST


def padded(cells, sides, width):
    for axis, dim in sides:
        count = lax.axis_size(axis)
        head = lax.slice_in_dim(cells, 0, width, axis=dim)
        tail = lax.slice_in_dim(cells, cells.shape[dim] - width, cells.shape[dim], axis=dim)
        cells = jnp.concatenate(
            [
                lax.ppermute(tail, axis, [(i, (i + 1) % count) for i in range(count)]),
                cells,
                lax.ppermute(head, axis, [((i + 1) % count, i) for i in range(count)]),
            ],
            axis=dim,
        )
    return cells


def passed_along(block, axis, distance):
    devices = range(lax.axis_size(axis))
    route = [((i - distance) % len(devices), i) for i in devices]
    return lax.ppermute(block, axis, route)


def sine_table(points):
    index = jnp.arange(points, dtype=jnp.int32) + 1
    reduced = index[:, None] * index[None, :] % (2 * (points + 1))
    return jnp.sin(math.pi * reduced.astype(jnp.float32) / (points + 1.0))


def eigen_values(position, points):
    return 2.0 - 2.0 * jnp.cos(math.pi * (position + 1.0) / (points + 1.0))


def kernel_rows(first_row, row_count):
    along_z = eigen_values(jnp.arange(NZ, dtype=jnp.float32), NZ)
    along_y = eigen_values(jnp.arange(row_count, dtype=jnp.float32) + first_row, NY)
    along_x = eigen_values(jnp.arange(NX, dtype=jnp.float32), NX)
    factor = 32.0 * math.pi / ((NZ + 1.0) * (NY + 1.0) * (NX + 1.0))
    return factor / (
        along_z[:, None, None] + along_y[None, :, None] + along_x[None, None, :] + MU_SQUARED
    )


def screened_potentials(densities):
    table_x = sine_table(NX)
    table_y = sine_table(NY)
    table_z = sine_table(NZ)
    row_count = NY // lax.axis_size("slab")
    kernel = kernel_rows((lax.axis_index("slab") * row_count).astype(jnp.float32), row_count)
    sectioned = jnp.einsum(
        "pzyx,xk->pzyk", densities, table_x, precision=HIGHEST, preferred_element_type=jnp.float32
    )
    sectioned = jnp.einsum(
        "pzyk,yj->pzjk", sectioned, table_y, precision=HIGHEST, preferred_element_type=jnp.float32
    )
    spectrum = (
        jnp.einsum(
            "pzjk,zi->pijk",
            lax.all_to_all(sectioned, "slab", split_axis=2, concat_axis=1, tiled=True),
            table_z,
            precision=HIGHEST,
            preferred_element_type=jnp.float32,
        )
        * kernel
    )
    inverse_z = jnp.einsum(
        "pijk,iz->pzjk", spectrum, table_z, precision=HIGHEST, preferred_element_type=jnp.float32
    )
    returned = lax.all_to_all(inverse_z, "slab", split_axis=1, concat_axis=2, tiled=True)
    sectioned = jnp.einsum(
        "pzjk,jy->pzyk", returned, table_y, precision=HIGHEST, preferred_element_type=jnp.float32
    )
    return jnp.einsum(
        "pzyk,kx->pzyx", sectioned, table_x, precision=HIGHEST, preferred_element_type=jnp.float32
    )


def pick_band(bands, which):
    return lax.dynamic_index_in_dim(bands, which, 0, keepdims=False)


def pair_density(left_field, right_field):
    return left_field * right_field


def add_into(summed, which, contrib):
    current = lax.dynamic_index_in_dim(summed, which, 0, keepdims=False)
    return lax.dynamic_update_index_in_dim(summed, current + contrib, which, 0)


def local(orbitals, plan):
    band_dev = orbitals.shape[0]
    block_count = lax.axis_size("band")
    band_index = lax.axis_index("band")
    mine = pick_band(plan, band_index)
    summed = jnp.zeros(orbitals.shape, jnp.float32)
    beside = padded(orbitals, (("band", 0),), band_dev)
    left_block = beside[:band_dev]
    right_block = beside[2 * band_dev :]
    densities = []
    own_bands = []
    partner_fields = []
    for side_slot, neighbour in ((0, left_block), (1, right_block)):
        for slot in range(band_dev):
            code_here = mine[side_slot, slot]
            own_band = code_here // band_dev
            partner = pick_band(neighbour, code_here % band_dev)
            own_field = pick_band(orbitals, own_band)
            if side_slot == 0:
                densities.append(pair_density(partner, own_field))
            else:
                densities.append(pair_density(own_field, partner))
            own_bands.append(own_band)
            partner_fields.append(partner)
    potentials = screened_potentials(jnp.stack(densities))
    for slot in range(2 * band_dev):
        summed = add_into(summed, own_bands[slot], potentials[slot] * partner_fields[slot])
    from_above = passed_along(potentials[:band_dev], "band", -1)
    from_below = passed_along(potentials[band_dev:], "band", 1)
    above_codes = pick_band(plan, (band_index + 1) % block_count)[0]
    below_codes = pick_band(plan, (band_index + block_count - 1) % block_count)[1]
    for slot in range(band_dev):
        code_above = above_codes[slot]
        summed = add_into(
            summed,
            code_above % band_dev,
            from_above[slot] * pick_band(right_block, code_above // band_dev),
        )
        code_below = below_codes[slot]
        summed = add_into(
            summed,
            code_below % band_dev,
            from_below[slot] * pick_band(left_block, code_below // band_dev),
        )
    return -MIXING * summed


def solution(mesh):
    in_specs = (P("band", "slab", None, None), P())
    out_specs = P("band", "slab", None, None)
    return jax.shard_map(local, mesh=mesh, in_specs=in_specs, out_specs=out_specs, check_vma=False)
```

profile of v0, /device:TPU:6, one launch (start us, length us, event | category | flops | bytes accessed | tf_op | source)
XLA Modules:
  0.0 302.1 jit_solution(16387058685978670167)
XLA Ops:
  0.0 4.3 %collective-permute-start = (f32[2,10,160,128]{3,2,1,0:T(8,128)}, f32[2,10,160,128]{3,2,1,0:T(8,128)S(1)}, u32[]{:S(2)}, u32[]{:S(2)}) collective-permute-start(f32[2,10,160,128]{3,2,1,0:T(8,128)} %param.2), channel_id=1, source_target_pairs={{0,16},{16,32},{32,48},{48,64},{64,80},{80,96},{96,112},{112,128},... | collective-permute-start | bytes 4915208 | tf_op jit(solution)/shard_map/ppermute | solution.py:25
  4.3 11.6 %collective-permute-start.1 = (f32[2,10,160,128]{3,2,1,0:T(8,128)}, f32[2,10,160,128]{3,2,1,0:T(8,128)S(1)}, u32[]{:S(2)}, u32[]{:S(2)}) collective-permute-start(f32[2,10,160,128]{3,2,1,0:T(8,128)} %param.2), channel_id=1, source_target_pairs={{16,0},{32,16},{48,32},{64,48},{80,64},{96,80},{112,96},{128,112},... | collective-permute-start | bytes 4915208 | tf_op jit(solution)/shard_map/ppermute | solution.py:27
  15.9 0.9 fusion.92
  16.8 0.6 fusion.108
  27.4 22.6 %collective-permute-done = f32[2,10,160,128]{3,2,1,0:T(8,128)S(1)} collective-permute-done((f32[2,10,160,128]{3,2,1,0:T(8,128)}, f32[2,10,160,128]{3,2,1,0:T(8,128)S(1)}, u32[]{:S(2)}, u32[]{:S(2)}) %collective-permute-start) | collective-permute-done | bytes 1638432 | tf_op jit(solution)/shard_map/ppermute | solution.py:25
  50.0 0.0 copy-start
  50.0 1.3 collective-permute-done.1
  51.3 0.0 copy-start.2
  51.3 2.9 dynamic-slice_multiply_fusion.3
  54.2 0.0 copy-done
  54.2 0.0 copy-done.2
  54.2 3.2 %fusion = f32[4,10,160,128]{3,2,1,0:T(8,128)S(1)} fusion(f32[1,10,160,128]{3,2,1,0:T(8,128)S(1)} %get-tuple-element.11, f32[1,10,160,128]{3,2,1,0:T(8,128)S(1)} %get-tuple-element.12, f32[1,10,160,128]{3,2,1,0:T(8,128)S(1)} %get-tuple-element.8, f32[1,10,160,128]{3,2,1,0:T(8,128)S(1)} %get-tuple-element.7, s32[128]{0:T(128)S(1)} %iota_add_fusion.1), kind=kOutput, calls=%fused_computation | convolution fusion | flops 1260896256 | bytes 6554112 | tf_op jit(solution)/shard_map/pzyx,xk->pzyk/dot_general | solution.py:66
  57.4 3.8 %convolution_bitcast_fusion = f32[4,10,160,128]{3,2,1,0:T(8,128)S(1)} fusion(f32[4,10,160,128]{3,2,1,0:T(8,128)S(1)} %fusion, s32[160]{0:T(256)S(1)} %iota_add_fusion), kind=kOutput, calls=%fused_computation.17 | convolution fusion | flops 1573094400 | bytes 6554240 | tf_op jit(solution)/shard_map/pzyk,yj->pzjk/dot_general | solution.py:69
  61.3 3.8 %copy.15 = f32[4,10,160,128]{3,0,1,2:T(4,128)} copy(f32[4,10,160,128]{3,2,1,0:T(8,128)S(1)} %convolution_bitcast_fusion) | data formatting | bytes 6553600 | tf_op jit(solution)/shard_map/pzyk,yj->pzjk/transpose | solution.py:69
  65.1 7.4 %all-to-all-start = ((f32[4,10,160,128]{3,0,1,2:T(4,128)}), f32[4,10,160,128]{3,0,1,2:T(4,128)S(1)}, u32[]{:S(2)}, u32[]{:S(2)}) async-start(f32[4,10,160,128]{3,0,1,2:T(4,128)} %copy.15), calls=%async_computation | async-start | bytes 6553600 | tf_op jit(solution)/shard_map/all_to_all | solution.py:75
  72.5 0.1 multiply_subtract_fusion.2
  72.6 0.1 broadcast_add_fusion
  72.7 1.2 add_divide_fusion
  73.9 52.9 %all-to-all-done = f32[4,10,160,128]{3,0,1,2:T(4,128)S(1)} async-done(((f32[4,10,160,128]{3,0,1,2:T(4,128)}), f32[4,10,160,128]{3,0,1,2:T(4,128)S(1)}, u32[]{:S(2)}, u32[]{:S(2)}) %all-to-all-start) | async-done | bytes 3276832 | tf_op jit(solution)/shard_map/all_to_all | solution.py:75
  126.7 0.6 copy.17
  127.3 0.0 copy-start.4
  127.3 4.0 %fusion.14 = f32[160,4,10,128]{3,0,2,1:T(8,128)S(1)} fusion(f32[4,160,10,128]{3,0,2,1:T(4,128)S(1)} %bitcast.45, s32[160]{0:T(256)S(1)} %iota_add_fusion), kind=kOutput, calls=%fused_computation.14 | convolution fusion | flops 1573094400 | bytes 6554240 | tf_op jit(solution)/shard_map/pzjk,zi->pijk/dot_general | solution.py:73
  131.3 0.0 copy-done.4
  131.3 3.7 %fusion.17 = f32[4,160,10,128]{3,1,2,0:T(8,128)S(1)} fusion(f32[160,4,10,128]{3,0,2,1:T(8,128)S(1)} %fusion.14, f32[160,10,128]{2,0,1:T(8,128)S(1)} %copy-done.4, s32[160]{0:T(256)S(1)} %iota_add_fusion), kind=kOutput, calls=%fused_computation.18 | convolution fusion | flops 1573913600 | bytes 7373440 | tf_op jit(solution)/shard_map/pijk,iz->pzjk/dot_general | solution.py:82
  135.1 2.1 copy.19
  137.2 70.1 %all_to_all.36 = f32[4,160,10,128]{3,0,2,1:T(4,128)S(1)} all-to-all(f32[4,160,10,128]{3,0,2,1:T(4,128)S(1)} %copy.19), channel_id=1, replica_groups=mesh['band'=32,'slab'=16] {'slab'}, dimensions={1} | all-to-all | bytes 6553600 | tf_op jit(solution)/shard_map/all_to_all | solution.py:85
  207.3 0.7 copy.20
  208.0 3.8 %fusion.12 = f32[160,4,10,128]{3,0,2,1:T(8,128)S(1)} fusion(f32[4,10,160,128]{3,0,2,1:T(4,128)S(1)} %bitcast.44, s32[160]{0:T(256)S(1)} %iota_add_fusion), kind=kOutput, calls=%fused_computation.12 | convolution fusion | flops 1573094400 | bytes 6554240 | tf_op jit(solution)/shard_map/pzjk,jy->pzyk/dot_general | solution.py:86
  211.8 3.0 fusion.8
  214.8 0.0 copy-start.5
  214.8 2.0 fusion.106
  216.8 36.3 %collective-permute-start.2 = (f32[2,10,160,128]{3,2,1,0:T(8,128)}, f32[2,10,160,128]{3,2,1,0:T(8,128)}, u32[]{:S(2)}, u32[]{:S(2)}) collective-permute-start(f32[2,10,160,128]{3,2,1,0:T(8,128)} %get-tuple-element.6), channel_id=1, source_target_pairs={{16,0},{32,16},{48,32},{64,48},{80,64},{96,80},{112,96},{128,112},... | collective-permute-start | bytes 4915208 | tf_op jit(solution)/shard_map/ppermute | solution.py:37
  253.1 1.9 collective-permute-start.3
  255.1 0.0 copy-done.5
  255.1 0.7 fusion.107
  265.5 0.0 copy-start.1
  265.5 0.2 broadcast_in_dim.10
  265.7 1.3 copy-done.1
  267.0 0.1 fusion.35
  267.1 0.0 copy-start.3
  267.1 0.2 fusion.34
  267.3 1.2 copy-done.3
  268.5 0.2 fusion.32
  268.7 0.2 fusion.30
  268.9 19.7 %collective-permute-done.2 = f32[2,10,160,128]{3,2,1,0:T(8,128)} collective-permute-done((f32[2,10,160,128]{3,2,1,0:T(8,128)}, f32[2,10,160,128]{3,2,1,0:T(8,128)}, u32[]{:S(2)}, u32[]{:S(2)}) %collective-permute-start.2) | collective-permute-done | bytes 1638432 | tf_op jit(solution)/shard_map/ppermute | solution.py:37
  288.7 1.3 fusion.28
  290.0 6.7 %collective-permute-done.3 = f32[2,10,160,128]{3,2,1,0:T(8,128)} collective-permute-done((f32[2,10,160,128]{3,2,1,0:T(8,128)}, f32[2,10,160,128]{3,2,1,0:T(8,128)}, u32[]{:S(2)}, u32[]{:S(2)}) %collective-permute-start.3) | collective-permute-done | bytes 1638432 | tf_op jit(solution)/shard_map/ppermute | solution.py:37
  296.7 1.3 fusion.26
  298.0 1.4 fusion.24
  299.4 1.4 fusion.22
  300.8 1.3 broadcast_multiply_fusion
  (4 shorter events, 0.1 us)
Async XLA Ops:
  0.0 50.0 %collective-permute-start = (f32[2,10,160,128]{3,2,1,0:T(8,128)}, f32[2,10,160,128]{3,2,1,0:T(8,128)S(1)}, u32[]{:S(2)}, u32[]{:S(2)}) collective-permute-start(f32[2,10,160,128]{3,2,1,0:T(8,128)} %param.2), channel_id=1, source_target_pairs={{0,16},{16,32},{32,48},{48,64},{64,80},{80,96},{96,112},{112,128},... | collective-permute-start | bytes 4915208 | tf_op jit(solution)/shard_map/ppermute | solution.py:25
  4.3 47.0 %collective-permute-start.1 = (f32[2,10,160,128]{3,2,1,0:T(8,128)}, f32[2,10,160,128]{3,2,1,0:T(8,128)S(1)}, u32[]{:S(2)}, u32[]{:S(2)}) collective-permute-start(f32[2,10,160,128]{3,2,1,0:T(8,128)} %param.2), channel_id=1, source_target_pairs={{16,0},{32,16},{48,32},{64,48},{80,64},{96,80},{112,96},{128,112},... | collective-permute-start | bytes 4915208 | tf_op jit(solution)/shard_map/ppermute | solution.py:27
  50.0 4.2 %copy-start = (f32[2,10,160,128]{3,2,1,0:T(8,128)}, f32[2,10,160,128]{3,2,1,0:T(8,128)S(1)}, u32[]{:S(2)}) copy-start(f32[2,10,160,128]{3,2,1,0:T(8,128)S(1)} %collective-permute-done) | copy-start | bytes 4915204
  51.3 2.9 copy-start.2
  65.1 61.7 %all-to-all-start = ((f32[4,10,160,128]{3,0,1,2:T(4,128)}), f32[4,10,160,128]{3,0,1,2:T(4,128)S(1)}, u32[]{:S(2)}, u32[]{:S(2)}) async-start(f32[4,10,160,128]{3,0,1,2:T(4,128)} %copy.15), calls=%async_computation | async-start | bytes 6553600 | tf_op jit(solution)/shard_map/all_to_all | solution.py:75
  127.3 4.0 %copy-start.4 = (f32[160,10,128]{2,0,1:T(8,128)S(1)}, f32[160,10,128]{2,0,1:T(8,128)}, u32[]{:S(2)}) copy-start(f32[160,10,128]{2,0,1:T(8,128)} %add_divide_fusion) | copy-start | bytes 2457604
  214.8 40.3 %copy-start.5 = (s32[32,2,2]{0,2,1:T(2,128)S(1)}, s32[32,2,2]{0,2,1:T(2,128)}, u32[]{:S(2)}) copy-start(s32[32,2,2]{0,2,1:T(2,128)} %param.3) | copy-start | bytes 1540
  216.8 71.8 %collective-permute-start.2 = (f32[2,10,160,128]{3,2,1,0:T(8,128)}, f32[2,10,160,128]{3,2,1,0:T(8,128)}, u32[]{:S(2)}, u32[]{:S(2)}) collective-permute-start(f32[2,10,160,128]{3,2,1,0:T(8,128)} %get-tuple-element.6), channel_id=1, source_target_pairs={{16,0},{32,16},{48,32},{64,48},{80,64},{96,80},{112,96},{128,112},... | collective-permute-start | bytes 4915208 | tf_op jit(solution)/shard_map/ppermute | solution.py:37
  253.1 43.6 %collective-permute-start.3 = (f32[2,10,160,128]{3,2,1,0:T(8,128)}, f32[2,10,160,128]{3,2,1,0:T(8,128)}, u32[]{:S(2)}, u32[]{:S(2)}) collective-permute-start(f32[2,10,160,128]{3,2,1,0:T(8,128)} %get-tuple-element.5), channel_id=1, source_target_pairs={{496,0},{0,16},{16,32},{32,48},{48,64},{64,80},{80,96},{96,112},{1... | collective-permute-start | bytes 4915208 | tf_op jit(solution)/shard_map/ppermute | solution.py:37
  265.5 1.4 copy-start.1
  267.1 1.4 copy-start.3
where the time goes:
time: 306 us; the launch traced here: 302 us
  waiting for transfers between devices  103 us (34%)
  blocking collectives  70.1 us (23%)
  starting transfers between devices  61.5 us (20%)
  matrix products  21.6 us (7%)
  between operations  20 us (7%)
  local copies, waits for them, and re-layouts  14 us (5%)
  other arithmetic  11.8 us (4%)
    all_to_all x1, blocking collectives, screened_potentials(): lax.all_to_all(inverse_z, 'slab', split_axis=1, concat_axis=2, tiled=True)  70.1 us
    all_to_all x1, waiting for transfers between devices, screened_potentials(): lax.all_to_all(sectioned, 'slab', split_axis=2, concat_axis=1, tiled=True)  52.9 us
    ppermute x2, starting transfers between devices, passed_along(): return lax.ppermute(block, axis, route)  38.2 us
    ppermute x2, waiting for transfers between devices, passed_along(): return lax.ppermute(block, axis, route)  26.4 us
    ppermute x1, waiting for transfers between devices, padded(): lax.ppermute(tail, axis, [(i, (i + 1) % count) for i in range(count)])  22.6 us
    ppermute x1, starting transfers between devices, padded(): lax.ppermute(head, axis, [((i + 1) % count, i) for i in range(count)])  11.6 us
    all_to_all x1, starting transfers between devices, screened_potentials(): lax.all_to_all(sectioned, 'slab', split_axis=2, concat_axis=1, tiled=True)  7.36 us
    dynamic_update_slice x8, other arithmetic, add_into(): return lax.dynamic_update_index_in_dim(summed, current + contrib, which, 0)  6.14 us
  transfers between devices with their start and end apart: 5, of which 5 were waited for; matrix products, arithmetic and copies ran while one was open for 2% of the time, Pallas kernels for 0%

commit v1 on v0

v1 whole, which is shorter than its diff:
```python
import functools
import math

import jax
import jax.numpy as jnp
import ml_dtypes
import numpy as np
from jax import lax
from jax.experimental import pallas as pl
from jax.experimental.pallas import tpu as pltpu
from jax.sharding import PartitionSpec as P

MU_SQUARED = 0.0025
MIXING = 0.25
CORES = 2
HALVES = 2
GROUP = 2
MESH = pl.DeviceIdType.MESH


def split_table(table):
    high = table.astype(ml_dtypes.bfloat16)
    low = (table - high.astype(np.float64)).astype(ml_dtypes.bfloat16)
    return high, low


def sine_table(points):
    index = np.arange(points, dtype=np.int64) + 1
    reduced = (index[:, None] * index[None, :]) % (2 * (points + 1))
    return np.sin(math.pi * reduced / (points + 1.0))


def eigen_values(points):
    return 2.0 - 2.0 * np.cos(math.pi * (np.arange(points) + 1.0) / (points + 1.0))


def constants(planes, total_planes, rows, points):
    high, low = split_table(sine_table(points))
    along_x = np.block([[high, low], [high, low]])
    high, low = split_table(sine_table(rows))
    along_y = np.concatenate([high, low], axis=0)
    shift = eigen_values(rows)[:, None] + eigen_values(points)[None, :] + MU_SQUARED
    root = np.sqrt(shift + shift * shift / 4.0)
    decay = 1.0 / (1.0 + shift / 2.0 + root)
    factor = 32.0 * math.pi / ((total_planes + 1.0) * (rows + 1.0) * (points + 1.0))
    scale = factor * (total_planes + 1.0) / 2.0 / (2.0 * root)
    modes = np.stack(
        [
            decay,
            decay**planes,
            decay ** (total_planes // 2),
            decay ** (total_planes + 1),
            1.0 / (1.0 - decay ** (2 * (total_planes + 1))),
            scale,
        ]
    ).astype(np.float32)
    return along_x, along_y, modes


def halves(block):
    high = block.astype(jnp.bfloat16)
    low = (block - high.astype(jnp.float32)).astype(jnp.bfloat16)
    return jnp.concatenate([high, low], axis=1)


def times_x(block, table):
    width = block.shape[1]
    product = jnp.dot(halves(block), table, preferred_element_type=jnp.float32)
    return product[:, :width] + product[:, width:]


def times_y(table, block):
    rows, width = block.shape
    product = jnp.dot(table, halves(block), preferred_element_type=jnp.float32)
    return (product[:rows, :width] + product[rows:, :width]) + (
        product[:rows, width:] + product[rows:, width:]
    )


def kernel(
    bands, slabs, plan, own, along_x, along_y, modes, out,
    part, field, given, taken, to_owner, at_owner, from_owner, at_member, mine, other,
    in_send, in_recv, owner_send, owner_recv, half_send, half_recv,
    member_send, member_recv, out_send, out_recv,
):
    band_dev, planes, rows, _ = own.shape
    members = slabs // HALVES
    chunk = band_dev * rows // members
    per_field = rows // chunk
    groups = planes // GROUP

    band = lax.axis_index("band")
    slab = lax.axis_index("slab")
    core = lax.rem(slab, CORES)
    half = slab // members
    me = lax.rem(slab, members)

    ahead = lax.rem(band + 1, bands)
    behind = lax.rem(band + bands - 1, bands)
    partner = jnp.where(core == 0, ahead, behind)
    giver = jnp.where(core == 0, behind, ahead)
    partner_id = {"band": partner, "slab": slab}
    giver_id = {"band": giver, "slab": slab}
    across_id = {"band": band, "slab": lax.rem(slab + members, slabs)}

    def member_id(member):
        same = lax.rem(member, CORES) == core
        return {"band": jnp.where(same, band, partner), "slab": half * members + member}

    barrier = pltpu.get_barrier_semaphore()
    everyone = [partner_id, giver_id, across_id]
    everyone += [member_id(lax.rem(me + k, members)) for k in range(1, members)]
    for device in everyone:
        pl.semaphore_signal(barrier, inc=1, device_id=device, device_id_type=MESH)
    pl.semaphore_wait(barrier, len(everyone))

    def remote(source, target, send, recv, device):
        return pltpu.make_async_remote_copy(
            src_ref=source, dst_ref=target, send_sem=send, recv_sem=recv,
            device_id=device, device_id_type=MESH,
        )

    def in_copy(c, g):
        span = pl.ds(g * GROUP, GROUP)
        return remote(
            own.at[c, span], part.at[c, span], in_send.at[c, g], in_recv.at[c, g], giver_id
        )

    def out_copy(c, g):
        span = pl.ds(g * GROUP, GROUP)
        return remote(
            given.at[c, span], taken.at[c, span], out_send.at[c, g], out_recv.at[c, g], partner_id
        )

    def owner_copy(c, k, slot):
        target = lax.rem(me + k, members)
        return remote(
            to_owner.at[c, target], at_owner.at[c, slot],
            owner_send.at[c, k], owner_recv.at[c, k], member_id(target),
        )

    def member_copy(c, k, slot):
        target = lax.rem(me + k, members)
        return remote(
            from_owner.at[c, target], at_member.at[c, slot],
            member_send.at[c, k], member_recv.at[c, k], member_id(target),
        )

    def half_copy(c):
        return remote(mine.at[c], other.at[c], half_send.at[c], half_recv.at[c], across_id)

    for c in range(band_dev):
        for g in range(groups):
            in_copy(c, g).start()

    edge = jnp.where(core == 0, band, behind)
    after = lax.rem(edge + 1, bands)

    def pair(a, c):
        return jnp.where(core == 0, a, c), jnp.where(core == 0, c, a)

    def weight(a, c):
        first, second = pair(a, c)
        total = jnp.float32(0.0)
        for slot in range(band_dev):
            total += jnp.where(plan[edge, 1, slot] == band_dev * first + second, 1.0, 0.0)
            total += jnp.where(plan[after, 0, slot] == band_dev * second + first, 1.0, 0.0)
        return -MIXING * total

    weights = [[weight(a, c) for c in range(band_dev)] for a in range(band_dev)]

    def forward(c, g):
        in_copy(c, g).wait_recv()
        for step in range(GROUP):
            z = g * GROUP + step
            for a in range(band_dev):
                density = own[a, z] * part[c, z]
                x, y = pair(a, c)
                field[x, y, z] = times_y(along_y[...], times_x(density, along_x[...]))

    def summarise(c):
        def body(m, _):
            a = m // per_field
            span = pl.ds(pl.multiple_of(lax.rem(m, per_field) * chunk, 8), chunk)
            decay = modes[0, span]
            rising = field[c, a, 0, span]
            falling = field[c, a, planes - 1, span]
            for z in range(1, planes):
                rising = rising * decay + field[c, a, z, span]
                falling = falling * decay + field[c, a, planes - 1 - z, span]
            to_owner[c, m, 0] = rising
            to_owner[c, m, 1] = falling * decay
            return 0

        lax.fori_loop(0, members, body, 0)
        for k in range(1, members):
            owner_copy(c, k, me).start()
        at_owner[c, me] = to_owner[c, me]

    my_rows = pl.ds(pl.multiple_of(lax.rem(me, per_field) * chunk, 8), chunk)

    def combine(c):
        for k in range(1, members):
            owner_copy(c, k, lax.rem(me + members - k, members)).wait_recv()
        block_decay = modes[1, my_rows]
        rising = at_owner[c, 0, 0]
        falling = at_owner[c, members - 1, 1]
        for d in range(1, members):
            rising = rising * block_decay + at_owner[c, d, 0]
            falling = falling * block_decay + at_owner[c, members - 1 - d, 1]
        mine[c, 0] = rising
        mine[c, 1] = falling
        half_copy(c).start()

    def resolve(c):
        half_copy(c).wait_recv()
        decay, block_decay, half_decay = modes[0, my_rows], modes[1, my_rows], modes[2, my_rows]
        whole_decay, image = modes[3, my_rows], modes[4, my_rows]
        lower = half == 0
        rising_low = jnp.where(lower, mine[c, 0], other[c, 0])
        rising_up = jnp.where(lower, other[c, 0], mine[c, 0])
        falling_low = jnp.where(lower, mine[c, 1], other[c, 1])
        falling_up = jnp.where(lower, other[c, 1], mine[c, 1])
        at_start = falling_low + half_decay * falling_up
        at_end = decay * (rising_up + half_decay * rising_low)
        from_start = (whole_decay * at_end - at_start) * image
        from_end = decay * ((whole_decay * at_start - at_end) * image)
        rising = jnp.where(lower, from_start, half_decay * from_start + rising_low)
        falling = jnp.where(lower, half_decay * from_end + falling_up, from_end)
        for d in range(members):
            from_owner[c, d, 0] = rising
            from_owner[c, members - 1 - d, 1] = falling
            rising = rising * block_decay + at_owner[c, d, 0]
            falling = falling * block_decay + at_owner[c, members - 1 - d, 1]
        for k in range(1, members):
            member_copy(c, k, me).start()
        at_member[c, me] = from_owner[c, me]

    def solve(c):
        for k in range(1, members):
            member_copy(c, k, lax.rem(me + members - k, members)).wait_recv()

        def body(m, _):
            a = m // per_field
            for part_row in range(0, chunk, 8):
                span = pl.ds(pl.multiple_of(lax.rem(m, per_field) * chunk + part_row, 8), 8)
                decay, scale = modes[0, span], modes[5, span]
                source = [field[c, a, z, span] for z in range(planes)]
                falling = [None] * planes
                falling[planes - 1] = at_member[c, m, 1, pl.ds(part_row, 8)]
                for z in range(planes - 1, 0, -1):
                    falling[z - 1] = (falling[z] + source[z]) * decay
                rising = at_member[c, m, 0, pl.ds(part_row, 8)]
                for z in range(planes):
                    rising = rising * decay + source[z]
                    field[c, a, z, span] = (rising + falling[z]) * scale
            return 0

        lax.fori_loop(0, members, body, 0)

    def inverse(c, g):
        for step in range(GROUP):
            z = g * GROUP + step
            total = None
            for a in range(band_dev):
                x, y = pair(a, c)
                potential = times_x(times_y(along_y[...], field[x, y, z]), along_x[...])
                potential = potential * weights[a][c]
                term = potential * own[a, z]
                total = term if total is None else total + term
                mutual = potential * part[c, z]
                out[a, z] = mutual if c == 0 else out[a, z] + mutual
            given[c, z] = total
        out_copy(c, g).start()

    def loop(first, last, body):
        def step(g, _):
            body(g)
            return 0

        lax.fori_loop(first, last, step, 0)

    for c in range(band_dev):
        loop(0, groups, functools.partial(forward, c))
    for step in (summarise, combine, resolve, solve):
        for x in range(band_dev):
            step(x)
    for c in range(band_dev):
        loop(0, groups, functools.partial(inverse, c))

    def finish(c, g):
        out_copy(c, g).wait_recv()
        for step in range(GROUP):
            z = g * GROUP + step
            out[c, z] = out[c, z] + taken[c, z]

    for c in range(band_dev):
        loop(0, groups, functools.partial(finish, c))
    for c in range(band_dev):
        for g in range(groups):
            in_copy(c, g).wait_send()
            out_copy(c, g).wait_send()
        for k in range(1, members):
            owner_copy(c, k, me).wait_send()
            member_copy(c, k, me).wait_send()
        half_copy(c).wait_send()


def solution(mesh):
    bands, slabs = mesh.shape["band"], mesh.shape["slab"]

    def local(orbitals, plan):
        band_dev, planes, rows, points = orbitals.shape
        members = slabs // HALVES
        chunk = band_dev * rows // members
        groups = planes // GROUP
        along_x, along_y, modes = constants(planes, planes * slabs, rows, points)
        vmem = pl.BlockSpec(memory_space=pltpu.VMEM)
        f32 = jnp.float32
        field = pltpu.VMEM((band_dev, planes, rows, points), f32)
        exchanged = pltpu.VMEM((band_dev, members, 2, chunk, points), f32)
        return pl.pallas_call(
            functools.partial(kernel, bands, slabs),
            out_shape=jax.ShapeDtypeStruct(orbitals.shape, f32),
            in_specs=[pl.BlockSpec(memory_space=pltpu.SMEM)] + [vmem] * 4,
            out_specs=vmem,
            scratch_shapes=[
                field,
                pltpu.VMEM((band_dev, band_dev, planes, rows, points), f32),
                field,
                field,
                exchanged,
                exchanged,
                exchanged,
                exchanged,
                pltpu.VMEM((band_dev, 2, chunk, points), f32),
                pltpu.VMEM((band_dev, 2, chunk, points), f32),
                pltpu.SemaphoreType.DMA((band_dev, groups)),
                pltpu.SemaphoreType.DMA((band_dev, groups)),
                pltpu.SemaphoreType.DMA((band_dev, members)),
                pltpu.SemaphoreType.DMA((band_dev, members)),
                pltpu.SemaphoreType.DMA((band_dev,)),
                pltpu.SemaphoreType.DMA((band_dev,)),
                pltpu.SemaphoreType.DMA((band_dev, members)),
                pltpu.SemaphoreType.DMA((band_dev, members)),
                pltpu.SemaphoreType.DMA((band_dev, groups)),
                pltpu.SemaphoreType.DMA((band_dev, groups)),
            ],
            compiler_params=pltpu.CompilerParams(
                collective_id=0, has_side_effects=True, vmem_limit_bytes=48 * 2**20
            ),
            name="exchange",
        )(plan, orbitals, jnp.asarray(along_x), jnp.asarray(along_y), jnp.asarray(modes))

    in_specs = (P("band", "slab", None, None), P())
    out_specs = P("band", "slab", None, None)
    return jax.shard_map(local, mesh=mesh, in_specs=in_specs, out_specs=out_specs, check_vma=False)
```

time: 306 us -> 89 us (0.29); the launches traced: 302 us -> 88.1 us
  waiting for transfers between devices: 103 us -> 0 us
  Pallas kernels: 0 us -> 81.9 us
  blocking collectives: 70.1 us -> 0 us
  starting transfers between devices: 61.5 us -> 0 us
  matrix products: 21.6 us -> 0 us
  between operations: 20 us -> 0.02 us
  other arithmetic: 11.8 us -> 0 us
  local copies, waits for them, and re-layouts: 14 us -> 6.22 us
    pallas_call x0 -> x1, Pallas kernels: none -> 81.9 us  [local(): pl.pallas_call(functools.partial(kernel, bands, slabs), out_shape=jax.Sha...]
    all_to_all x1 -> x0, blocking collectives: 70.1 us -> none  [screened_potentials(): lax.all_to_all(inverse_z, 'slab', split_axis=1, concat_axis=2, tiled=True)]
    ppermute x4 -> x0, starting transfers between devices: 54.1 us -> none  [the longest x2 38.2 us: passed_along(): return lax.ppermute(block, axis, route)]
    all_to_all x1 -> x0, waiting for transfers between devices: 52.9 us -> none  [screened_potentials(): lax.all_to_all(sectioned, 'slab', split_axis=2, concat_axis=1, tiled=True)]
    ppermute x4 -> x0, waiting for transfers between devices: 50.2 us -> none  [the longest x2 26.4 us: passed_along(): return lax.ppermute(block, axis, route)]
    dot_general x6 -> x0, matrix products: 21.6 us -> none  [the longest x1 4.01 us: screened_potentials(): jnp.einsum('pzjk,zi->pijk', lax.all_to_all(sectioned, 'slab', split_axis=...]
    all_to_all x1 -> x0, starting transfers between devices: 7.36 us -> none  [screened_potentials(): lax.all_to_all(sectioned, 'slab', split_axis=2, concat_axis=1, tiled=True)]
    dynamic_update_slice x8 -> x0, other arithmetic: 6.14 us -> none  [add_into(): return lax.dynamic_update_index_in_dim(summed, current + contrib, which, 0)]
  transfers between devices with their start and end apart: 5 -> 0, of which waited for: 5 -> 0; matrix products, arithmetic and copies ran while one was open for 2% -> 0% of each run, Pallas kernels for 0% -> 0%
where the time goes in v1:
time: 89 us; the launch traced here: 88.1 us
  Pallas kernels  81.9 us (92%)
  local copies, waits for them, and re-layouts  6.22 us (7%)
    pallas_call x1, Pallas kernels, local(): pl.pallas_call(functools.partial(kernel, bands, slabs), out_shape=jax.Sha...  81.9 us
    unnamed x10, local copies, waits for them, and re-layouts  6.22 us

profile of v1, /device:TPU:6, one launch (start us, length us, event | category | flops | bytes accessed | tf_op | source)
XLA Modules:
  0.0 88.1 jit_solution(10527824348239991131)
XLA Ops:
  0.0 0.8 copy.6.plan
  0.8 0.0 copy-start
  0.8 1.4 %copy-done = f32[2,10,160,128]{3,2,1,0:T(8,128)S(1)} copy-done((f32[2,10,160,128]{3,2,1,0:T(8,128)S(1)}, f32[2,10,160,128]{3,2,1,0:T(8,128)}, u32[]{:S(2)}) %copy-start) | copy-done | bytes 1638424
  2.2 0.0 copy-start.1
  2.2 1.0 %copy-done.1 = f32[6,160,128]{2,1,0:T(8,128)S(1)} copy-done((f32[6,160,128]{2,1,0:T(8,128)S(1)}, f32[6,160,128]{2,1,0:T(8,128)}, u32[]{:S(2)}) %copy-start.1) | copy-done | bytes 491544
  3.2 0.0 copy-start.2
  3.2 0.9 %copy-done.2 = bf16[320,160]{1,0:T(8,128)(2,1)S(1)} copy-done((bf16[320,160]{1,0:T(8,128)(2,1)S(1)}, bf16[320,160]{1,0:T(8,128)(2,1)}, u32[]{:S(2)}) %copy-start.2) | copy-done | bytes 102424
  4.2 0.0 copy-start.3
  4.2 0.9 %copy-done.3 = bf16[256,256]{1,0:T(8,128)(2,1)S(1)} copy-done((bf16[256,256]{1,0:T(8,128)(2,1)S(1)}, bf16[256,256]{1,0:T(8,128)(2,1)}, u32[]{:S(2)}) %copy-start.3) | copy-done | bytes 131096
  5.1 81.9 %exchange.1 = f32[2,10,160,128]{3,2,1,0:T(8,128)S(1)} custom-call(s32[32,2,2]{2,1,0:T(2,128)S(1)} %copy.6.plan, f32[2,10,160,128]{3,2,1,0:T(8,128)S(1)} %copy-done, bf16[256,256]{1,0:T(8,128)(2,1)S(1)} %copy-done.3, bf16[320,160]{1,0:T(8,128)(2,1)S(1)} %copy-done.2, f32[6,160,128]{2,1,0:T(8,128)S(1)} %copy-done.1), custom_call_target="tpu_custom_call" | custom-call | tf_op jit(solution)/shard_map/exchange/pallas_call | solution.py:322
  87.0 1.2 %copy.8 = f32[2,10,160,128]{3,2,1,0:T(8,128)} copy(f32[2,10,160,128]{3,2,1,0:T(8,128)S(1)} %exchange.1) | data formatting | bytes 3276800
Async XLA Ops:
  0.8 1.4 %copy-start = (f32[2,10,160,128]{3,2,1,0:T(8,128)S(1)}, f32[2,10,160,128]{3,2,1,0:T(8,128)}, u32[]{:S(2)}) copy-start(f32[2,10,160,128]{3,2,1,0:T(8,128)} %own.1) | copy-start | bytes 4915204
  2.2 1.0 %copy-start.1 = (f32[6,160,128]{2,1,0:T(8,128)S(1)}, f32[6,160,128]{2,1,0:T(8,128)}, u32[]{:S(2)}) copy-start(f32[6,160,128]{2,1,0:T(8,128)} %constant.8.clone.modes) | copy-start | bytes 1474564
  3.2 0.9 %copy-start.2 = (bf16[320,160]{1,0:T(8,128)(2,1)S(1)}, bf16[320,160]{1,0:T(8,128)(2,1)}, u32[]{:S(2)}) copy-start(bf16[320,160]{1,0:T(8,128)(2,1)} %constant.7.clone.along_y) | copy-start | bytes 307204
  4.2 0.9 %copy-start.3 = (bf16[256,256]{1,0:T(8,128)(2,1)S(1)}, bf16[256,256]{1,0:T(8,128)(2,1)}, u32[]{:S(2)}) copy-start(bf16[256,256]{1,0:T(8,128)(2,1)} %constant.6.clone.along_x) | copy-start | bytes 393220

commit v2 on v1

v2 whole, which is shorter than its diff:
```python
import functools
import math

import jax
import jax.numpy as jnp
import numpy as np
from jax import lax
from jax.experimental import pallas as pl
from jax.experimental.pallas import tpu as pltpu
from jax.sharding import PartitionSpec as P

MU_SQUARED = 0.0025
MIXING = 0.25
CORES = 2
HALVES = 2
GROUP = 2
MESH = pl.DeviceIdType.MESH


def sine_table(points):
    index = np.arange(points, dtype=np.int64) + 1
    reduced = (index[:, None] * index[None, :]) % (2 * (points + 1))
    return np.sin(math.pi * reduced / (points + 1.0))


def eigen_values(points):
    return 2.0 - 2.0 * np.cos(math.pi * (np.arange(points) + 1.0) / (points + 1.0))


def constants(planes, total_planes, rows, points):
    table_x = sine_table(points).astype(np.float32)
    table_y = sine_table(rows).astype(np.float32)
    shift = eigen_values(rows)[:, None] + eigen_values(points)[None, :] + MU_SQUARED
    root = np.sqrt(shift + shift * shift / 4.0)
    decay = 1.0 / (1.0 + shift / 2.0 + root)
    factor = 32.0 * math.pi / ((total_planes + 1.0) * (rows + 1.0) * (points + 1.0))
    scale = factor * (total_planes + 1.0) / 2.0 / (2.0 * root)
    modes = np.stack(
        [
            decay,
            decay**planes,
            decay ** (total_planes // 2),
            1.0 / (1.0 - decay ** (2 * (total_planes + 1))),
            scale,
        ]
    ).astype(np.float32)
    return table_x, table_y, modes


def split(block):
    high = block.astype(jnp.bfloat16)
    low = (block - high.astype(jnp.float32)).astype(jnp.bfloat16)
    return high, low


def halves(block):
    return jnp.concatenate(split(block), axis=1)


def times_x(block, table):
    width = block.shape[1]
    product = jnp.dot(halves(block), table, preferred_element_type=jnp.float32)
    return product[:, :width] + product[:, width:]


def times_y(table, block):
    rows, width = block.shape
    product = jnp.dot(table, halves(block), preferred_element_type=jnp.float32)
    return (product[:rows, :width] + product[rows:, :width]) + (
        product[:rows, width:] + product[rows:, width:]
    )


def kernel(
    bands, slabs, plan_hbm, orbitals, table_x_hbm, table_y_hbm, modes_hbm, out, taken,
    plan, own, table_x, table_y, modes, along_x, along_y,
    part, field, given, summary, at_owner, from_owner, at_member, outer, mine, other,
    load, in_send, in_recv, owner_send, owner_recv, half_send, half_recv,
    member_send, member_recv, out_send, out_recv,
):
    band_dev, planes, rows, points = own.shape
    members = slabs // HALVES
    chips = members // CORES
    chunk = rows // chips
    groups = planes // GROUP

    loads = [
        pltpu.make_async_copy(source, target, load.at[i])
        for i, (source, target) in enumerate(
            [
                (table_x_hbm, table_x),
                (table_y_hbm, table_y),
                (modes_hbm, modes),
                (plan_hbm, plan),
                (orbitals, own),
            ]
        )
    ]
    for copy in loads:
        copy.start()

    band = lax.axis_index("band")
    slab = lax.axis_index("slab")
    core = lax.rem(slab, CORES)
    half = slab // members
    me = lax.rem(slab, members)
    chip = me // CORES
    lower = half == 0

    ahead = lax.rem(band + 1, bands)
    behind = lax.rem(band + bands - 1, bands)
    partner = jnp.where(core == 0, ahead, behind)
    giver = jnp.where(core == 0, behind, ahead)
    partner_id = {"band": partner, "slab": slab}
    giver_id = {"band": giver, "slab": slab}
    across_id = {"band": band, "slab": lax.rem(slab + members, slabs)}

    def member_id(member):
        same = lax.rem(member, CORES) == core
        return {"band": jnp.where(same, band, partner), "slab": half * members + member}

    barrier = pltpu.get_barrier_semaphore()
    everyone = [partner_id, giver_id, across_id]
    everyone += [member_id(lax.rem(me + k, members)) for k in range(1, members)]
    for device in everyone:
        pl.semaphore_signal(barrier, inc=1, device_id=device, device_id_type=MESH)
    pl.semaphore_wait(barrier, len(everyone))

    def remote(source, target, send, recv, device):
        return pltpu.make_async_remote_copy(
            src_ref=source, dst_ref=target, send_sem=send, recv_sem=recv,
            device_id=device, device_id_type=MESH,
        )

    def in_copy(c, g):
        span = pl.ds(g * GROUP, GROUP)
        return remote(
            orbitals.at[c, span], part.at[c, span], in_send.at[c, g], in_recv.at[c, g], giver_id
        )

    def out_copy(c, g):
        span = pl.ds(g * GROUP, GROUP)
        return remote(
            given.at[c, span], taken.at[c, span], out_send.at[c, g], out_recv.at[c, g], partner_id
        )

    def pair(side, a, c):
        return jnp.where(side == 0, a, c), jnp.where(side == 0, c, a)

    def owner_copy(a, c, j):
        target = lax.rem(chip + j, chips)
        slot, _ = pair(core, a, c)
        return remote(
            summary.at[a, c, target], at_owner.at[slot, me], owner_send.at[a, c, j],
            owner_recv.at[slot, core ^ a ^ c, j], member_id(target * CORES + (a ^ c)),
        )

    def owner_wait(t):
        for other_core in range(CORES):
            for j in range(1 - other_core, chips):
                source = lax.rem(chip + chips - j, chips) * CORES + (core ^ other_core)
                remote(
                    summary.at[0, 0, 0], at_owner.at[t, source], owner_send.at[0, 0, j],
                    owner_recv.at[t, other_core, j], member_id(source),
                ).wait_recv()

    def member_copy(t, other_core, j):
        target = lax.rem(chip + j, chips) * CORES + (core ^ other_core)
        return remote(
            from_owner.at[t, target], at_member.at[core, t, chip],
            member_send.at[t, other_core, j], member_recv.at[core, t, j], member_id(target),
        )

    def member_wait(a, c):
        slot, _ = pair(core, a, c)
        owner = a ^ c

        def wait(j):
            source = lax.rem(chip + chips - j, chips)
            remote(
                from_owner.at[0, 0], at_member.at[owner, slot, source], member_send.at[0, 0, j],
                member_recv.at[owner, slot, j], member_id(source * CORES + owner),
            ).wait_recv()

        pl.when(core != owner)(lambda: wait(0))
        for j in range(1, chips):
            wait(j)

    def half_copy(t):
        return remote(mine.at[t], other.at[t], half_send.at[t], half_recv.at[t], across_id)

    for c in range(band_dev):
        for g in range(groups):
            in_copy(c, g).start()
    for copy in loads:
        copy.wait()
    high, low = split(table_x[...])
    for row in (0, points):
        along_x[pl.ds(row, points), pl.ds(0, points)] = high
        along_x[pl.ds(row, points), pl.ds(points, points)] = low
    high, low = split(table_y[...])
    along_y[pl.ds(0, rows)] = high
    along_y[pl.ds(rows, rows)] = low

    edge = jnp.where(core == 0, band, behind)
    after = lax.rem(edge + 1, bands)

    def weight(a, c):
        first, second = pair(core, a, c)
        total = jnp.float32(0.0)
        for slot in range(band_dev):
            total += jnp.where(plan[1, slot, edge] == band_dev * first + second, 1.0, 0.0)
            total += jnp.where(plan[0, slot, after] == band_dev * second + first, 1.0, 0.0)
        return -MIXING * total

    weights = [[weight(a, c) for c in range(band_dev)] for a in range(band_dev)]

    def forward(c, g):
        in_copy(c, g).wait_recv()
        for step in range(GROUP):
            z = g * GROUP + step
            for a in range(band_dev):
                density = own[a, z] * part[c, z]
                field[c, a, z] = times_y(along_y[...], times_x(density, along_x[...]))

    def summarise(a, c):
        def body(i, _):
            span = pl.ds(pl.multiple_of(i * chunk, 8), chunk)
            decay = modes[0, span]
            rising = field[c, a, 0, span]
            falling = field[c, a, planes - 1, span]
            for z in range(1, planes):
                rising = rising * decay + field[c, a, z, span]
                falling = falling * decay + field[c, a, planes - 1 - z, span]
            summary[a, c, i, 0] = rising
            summary[a, c, i, 1] = falling * decay
            return 0

        lax.fori_loop(0, chips, body, 0)
        for j in range(1, chips):
            owner_copy(a, c, j).start()
        pl.when(core != a ^ c)(lambda: owner_copy(a, c, 0).start())

        @pl.when(core == a ^ c)
        def _():
            slot, _ = pair(core, a, c)
            at_owner[slot, me] = summary[a, c, chip]

    my_rows = pl.ds(pl.multiple_of(chip * chunk, 8), chunk)

    def toward(decay):
        square = decay * decay
        return jnp.where(lower, 1.0, square), jnp.where(lower, square, 1.0)

    def combine(t):
        block_decay = modes[1, my_rows]
        rising = at_owner[t, 0, 0]
        falling = at_owner[t, members - 1, 1]
        for d in range(1, members):
            rising = rising * block_decay + at_owner[t, d, 0]
            falling = falling * block_decay + at_owner[t, members - 1 - d, 1]
        here, _ = toward(modes[0, my_rows])
        outward = jnp.where(lower, falling, rising)
        outer[t] = outward
        mine[t] = jnp.where(lower, rising, falling) - here * modes[2, my_rows] * outward
        half_copy(t).start()

    def resolve(t):
        half_copy(t).wait_recv()
        block_decay, half_decay, image = modes[1, my_rows], modes[2, my_rows], modes[3, my_rows]
        here, there = toward(modes[0, my_rows])
        inward = (other[t] - half_decay * half_decay * there * mine[t]) * image
        at_end = -here * (outer[t] + half_decay * inward)
        rising = jnp.where(lower, at_end, inward)
        falling = jnp.where(lower, inward, at_end)
        for d in range(members):
            from_owner[t, d, 0] = rising
            from_owner[t, members - 1 - d, 1] = falling
            rising = rising * block_decay + at_owner[t, d, 0]
            falling = falling * block_decay + at_owner[t, members - 1 - d, 1]
        at_member[core, t, chip] = from_owner[t, me]

    def send_back(t, other_core):
        for j in range(1 - other_core, chips):
            member_copy(t, other_core, j).start()

    def solve(c, a):
        slot, _ = pair(core, a, c)

        def body(i, _):
            for row in range(0, chunk, 8):
                span = pl.ds(pl.multiple_of(i * chunk + row, 8), 8)
                decay, scale = modes[0, span], modes[4, span]
                source = [field[c, a, z, span] for z in range(planes)]
                falling = [None] * planes
                falling[planes - 1] = at_member[a ^ c, slot, i, 1, pl.ds(row, 8)]
                for z in range(planes - 1, 0, -1):
                    falling[z - 1] = (falling[z] + source[z]) * decay
                rising = at_member[a ^ c, slot, i, 0, pl.ds(row, 8)]
                for z in range(planes):
                    rising = rising * decay + source[z]
                    field[c, a, z, span] = (rising + falling[z]) * scale
            return 0

        lax.fori_loop(0, chips, body, 0)

    def potential(c, a, z):
        return times_x(times_y(along_y[...], field[c, a, z]), along_x[...]) * weights[a][c]

    def first_potential(g):
        for step in range(GROUP):
            z = g * GROUP + step
            field[0, 0, z] = potential(0, 0, z)

    def inverse(c, g):
        for step in range(GROUP):
            z = g * GROUP + step
            total = None
            for a in range(band_dev):
                value = field[0, 0, z] if a == c == 0 else potential(c, a, z)
                term = value * own[a, z]
                total = term if total is None else total + term
                mutual = value * part[c, z]
                out[a, z] = mutual if c == 0 else out[a, z] + mutual
            given[c, z] = total
        out_copy(c, g).start()

    def loop(first, last, body):
        def step(g, _):
            body(g)
            return 0

        lax.fori_loop(first, last, step, 0)

    def settle(a, c):
        member_wait(a, c)
        solve(c, a)

    loop(0, groups, functools.partial(forward, 0))
    summarise(0, 0)
    summarise(1, 0)
    loop(0, groups - 2, functools.partial(forward, 1))

    @pl.when(core == 0)
    def _():
        owner_wait(0)
        combine(0)

    loop(groups - 2, groups - 1, functools.partial(forward, 1))

    loop(groups - 1, groups, functools.partial(forward, 1))
    summarise(0, 1)

    @pl.when(core == 0)
    def _():
        resolve(0)
        send_back(0, 0)
        send_back(0, 1)

    settle(0, 0)

    @pl.when(core == 1)
    def _():
        for t in range(band_dev):
            owner_wait(t)
            combine(t)
        summarise(1, 1)
        loop(0, groups, first_potential)
        resolve(1)
        send_back(1, 1)
        resolve(0)
        send_back(0, 0)
        send_back(1, 0)
        send_back(0, 1)

    @pl.when(core == 0)
    def _():
        loop(0, groups, first_potential)
        summarise(1, 1)
        owner_wait(1)
        combine(1)

    settle(1, 0)
    loop(0, 1, functools.partial(inverse, 0))

    @pl.when(core == 0)
    def _():
        resolve(1)
        send_back(1, 0)
        send_back(1, 1)

    loop(1, groups, functools.partial(inverse, 0))
    settle(0, 1)
    settle(1, 1)
    loop(0, groups, functools.partial(inverse, 1))

    for c in range(band_dev):
        for g in range(groups):
            in_copy(c, g).wait_send()
            out_copy(c, g).wait_send()
            out_copy(c, g).wait_recv()
        half_copy(c).wait_send()
        for a in range(band_dev):
            for j in range(1, chips):
                owner_copy(a, c, j).wait_send()
            pl.when(core != a ^ c)(owner_copy(a, c, 0).wait_send)
        for other_core in range(CORES):
            for j in range(1 - other_core, chips):
                member_copy(c, other_core, j).wait_send()


def solution(mesh):
    bands, slabs = mesh.shape["band"], mesh.shape["slab"]

    def local(orbitals, plan):
        band_dev, planes, rows, points = orbitals.shape
        members = slabs // HALVES
        chips = members // CORES
        chunk = rows // chips
        groups = planes // GROUP
        table_x, table_y, modes = constants(planes, planes * slabs, rows, points)
        plan = jnp.transpose(plan, (1, 2, 0))
        operands = (plan, orbitals, table_x, table_y, modes)
        f32 = jnp.float32
        field = pltpu.VMEM((band_dev, planes, rows, points), f32)
        edge = pltpu.VMEM((band_dev, chunk, points), f32)

        def semaphores(*shape):
            return [pltpu.SemaphoreType.DMA(shape)] * 2

        kept, taken = pl.pallas_call(
            functools.partial(kernel, bands, slabs),
            out_shape=[jax.ShapeDtypeStruct(orbitals.shape, f32)] * 2,
            in_specs=[pl.BlockSpec(memory_space=pltpu.HBM)] * 5,
            out_specs=[pl.BlockSpec(memory_space=pltpu.VMEM)] * 2,
            scratch_shapes=[
                pltpu.SMEM(plan.shape, plan.dtype),
                field,
                pltpu.VMEM(table_x.shape, f32),
                pltpu.VMEM(table_y.shape, f32),
                pltpu.VMEM(modes.shape, f32),
                pltpu.VMEM((2 * points, 2 * points), jnp.bfloat16),
                pltpu.VMEM((2 * rows, rows), jnp.bfloat16),
                field,
                pltpu.VMEM((band_dev, band_dev, planes, rows, points), f32),
                field,
                pltpu.VMEM((band_dev, band_dev, chips, 2, chunk, points), f32),
                pltpu.VMEM((band_dev, members, 2, chunk, points), f32),
                pltpu.VMEM((band_dev, members, 2, chunk, points), f32),
                pltpu.VMEM((CORES, band_dev, chips, 2, chunk, points), f32),
                edge,
                edge,
                edge,
                pltpu.SemaphoreType.DMA((5,)),
                *semaphores(band_dev, groups),
                *semaphores(band_dev, band_dev, chips),
                *semaphores(band_dev),
                *semaphores(CORES, band_dev, chips),
                *semaphores(band_dev, groups),
            ],
            compiler_params=pltpu.CompilerParams(
                collective_id=0, has_side_effects=True, vmem_limit_bytes=40 * 2**20
            ),
            name="exchange",
        )(*[pltpu.with_memory_space_constraint(jnp.asarray(x), pltpu.HBM) for x in operands])
        return kept + taken

    in_specs = (P("band", "slab", None, None), P())
    out_specs = P("band", "slab", None, None)
    return jax.shard_map(local, mesh=mesh, in_specs=in_specs, out_specs=out_specs, check_vma=False)
```

time: 89 us -> 86.2 us (0.969)
  local copies, waits for them, and re-layouts: 6.22 us -> 0 us
  Pallas kernels: 81.9 us -> 84.7 us
  other arithmetic: 0 us -> 1.34 us
    unnamed x10 -> x0, local copies, waits for them, and re-layouts: 6.22 us -> none
    pallas_call x1, Pallas kernels: 81.9 us -> 84.7 us  [local(): pl.pallas_call(functools.partial(kernel, bands, slabs), out_shape=[jax.Sh...]
    add x0 -> x1, other arithmetic: none -> 1.34 us  [local(): return kept + taken]
where the time goes in v2:
time: 86.2 us; the launch traced here: 86 us
  Pallas kernels  84.7 us (98%)
  other arithmetic  1.34 us (2%)
    pallas_call x1, Pallas kernels, local(): pl.pallas_call(functools.partial(kernel, bands, slabs), out_shape=[jax.Sh...  84.7 us

profile of v2, /device:TPU:6, one launch (start us, length us, event | category | flops | bytes accessed | tf_op | source)
XLA Modules:
  0.0 86.0 jit_solution(10102720454827255962)
XLA Ops:
  0.0 84.7 %exchange.1 = (f32[2,10,160,128]{3,2,1,0:T(8,128)S(1)}, f32[2,10,160,128]{3,2,1,0:T(8,128)S(1)}) custom-call(s32[2,2,32]{2,1,0:T(2,128)} %bitcast.1, f32[2,10,160,128]{3,2,1,0:T(8,128)} %orbitals.1, f32[128,128]{1,0:T(8,128)} %constant.6.clone.table_x_hbm, f32[160,160]{1,0:T(8,128)} %constant.7.clone.table_y_hbm, f32[5,160,128]{2,1,0:T(8,128)} %constant.8.clone.modes_hbm), custom_call_target="tpu_custom_call" | custom-call | tf_op jit(solution)/shard_map/exchange/pallas_call | solution.py:431
  84.7 1.3 %add.3 = f32[2,10,160,128]{3,2,1,0:T(8,128)} add(f32[2,10,160,128]{3,2,1,0:T(8,128)S(1)} %get-tuple-element.7, f32[2,10,160,128]{3,2,1,0:T(8,128)S(1)} %get-tuple-element.8) | non-fusion elementwise | flops 409600 | bytes 4915200 | tf_op jit(solution)/shard_map/add | solution.py:466

commit v3 on v2

--- a/solution.py
+++ b/solution.py
@@ -149,31 +149,31 @@
 
     def owner_copy(a, c, j):
         target = lax.rem(chip + j, chips)
-        slot, _ = pair(core, a, c)
+        slot, owner = pair(core, a, c)
         return remote(
             summary.at[a, c, target], at_owner.at[slot, me], owner_send.at[a, c, j],
-            owner_recv.at[slot, core ^ a ^ c, j], member_id(target * CORES + (a ^ c)),
+            owner_recv.at[slot, lax.rem(core + owner, CORES), j],
+            member_id(target * CORES + owner),
         )
 
     def owner_wait(t):
         for other_core in range(CORES):
             for j in range(1 - other_core, chips):
-                source = lax.rem(chip + chips - j, chips) * CORES + (core ^ other_core)
+                source = lax.rem(chip + chips - j, chips) * CORES + lax.rem(core + other_core, CORES)
                 remote(
                     summary.at[0, 0, 0], at_owner.at[t, source], owner_send.at[0, 0, j],
                     owner_recv.at[t, other_core, j], member_id(source),
                 ).wait_recv()
 
     def member_copy(t, other_core, j):
-        target = lax.rem(chip + j, chips) * CORES + (core ^ other_core)
+        target = lax.rem(chip + j, chips) * CORES + lax.rem(core + other_core, CORES)
         return remote(
             from_owner.at[t, target], at_member.at[core, t, chip],
             member_send.at[t, other_core, j], member_recv.at[core, t, j], member_id(target),
         )
 
     def member_wait(a, c):
-        slot, _ = pair(core, a, c)
-        owner = a ^ c
+        slot, owner = pair(core, a, c)
 
         def wait(j):
             source = lax.rem(chip + chips - j, chips)
@@ -239,11 +239,11 @@
         lax.fori_loop(0, chips, body, 0)
         for j in range(1, chips):
             owner_copy(a, c, j).start()
-        pl.when(core != a ^ c)(lambda: owner_copy(a, c, 0).start())
-
-        @pl.when(core == a ^ c)
+        slot, owner = pair(core, a, c)
+        pl.when(core != owner)(lambda: owner_copy(a, c, 0).start())
+
+        @pl.when(core == owner)
         def _():
-            slot, _ = pair(core, a, c)
             at_owner[slot, me] = summary[a, c, chip]
 
     my_rows = pl.ds(pl.multiple_of(chip * chunk, 8), chunk)
@@ -285,7 +285,7 @@
             member_copy(t, other_core, j).start()
 
     def solve(c, a):
-        slot, _ = pair(core, a, c)
+        slot, owner = pair(core, a, c)
 
         def body(i, _):
             for row in range(0, chunk, 8):
@@ -293,10 +293,10 @@
                 decay, scale = modes[0, span], modes[4, span]
                 source = [field[c, a, z, span] for z in range(planes)]
                 falling = [None] * planes
-                falling[planes - 1] = at_member[a ^ c, slot, i, 1, pl.ds(row, 8)]
+                falling[planes - 1] = at_member[owner, slot, i, 1, pl.ds(row, 8)]
                 for z in range(planes - 1, 0, -1):
                     falling[z - 1] = (falling[z] + source[z]) * decay
-                rising = at_member[a ^ c, slot, i, 0, pl.ds(row, 8)]
+                rising = at_member[owner, slot, i, 0, pl.ds(row, 8)]
                 for z in range(planes):
                     rising = rising * decay + source[z]
                     field[c, a, z, span] = (rising + falling[z]) * scale
@@ -336,6 +336,7 @@
         member_wait(a, c)
         solve(c, a)
 
+    late = 1 - core
     loop(0, groups, functools.partial(forward, 0))
     summarise(0, 0)
     summarise(1, 0)
@@ -346,44 +347,33 @@
         owner_wait(0)
         combine(0)
 
-    loop(groups - 2, groups - 1, functools.partial(forward, 1))
-
-    loop(groups - 1, groups, functools.partial(forward, 1))
+    loop(groups - 2, groups, functools.partial(forward, 1))
     summarise(0, 1)
 
     @pl.when(core == 0)
     def _():
         resolve(0)
+        send_back(0, 1)
         send_back(0, 0)
-        send_back(0, 1)
-
+
+    owner_wait(late)
+    combine(late)
+    summarise(1, 1)
     settle(0, 0)
+    loop(0, groups, first_potential)
+    resolve(late)
+    send_back(late, 0)
+    send_back(late, 1)
 
     @pl.when(core == 1)
     def _():
-        for t in range(band_dev):
-            owner_wait(t)
-            combine(t)
-        summarise(1, 1)
-        loop(0, groups, first_potential)
-        resolve(1)
-        send_back(1, 1)
-        resolve(0)
-        send_back(0, 0)
-        send_back(1, 0)
-        send_back(0, 1)
-
-    @pl.when(core == 0)
-    def _():
-        loop(0, groups, first_potential)
-        summarise(1, 1)
         owner_wait(1)
         combine(1)
 
     settle(1, 0)
     loop(0, 1, functools.partial(inverse, 0))
 
-    @pl.when(core == 0)
+    @pl.when(core == 1)
     def _():
         resolve(1)
         send_back(1, 0)
@@ -403,7 +393,8 @@
         for a in range(band_dev):
             for j in range(1, chips):
                 owner_copy(a, c, j).wait_send()
-            pl.when(core != a ^ c)(owner_copy(a, c, 0).wait_send)
+            _, owner = pair(core, a, c)
+            pl.when(core != owner)(owner_copy(a, c, 0).wait_send)
         for other_core in range(CORES):
             for j in range(1 - other_core, chips):
                 member_copy(c, other_core, j).wait_send()

time: 86.2 us -> 79.9 us (0.927)
  Pallas kernels: 84.7 us -> 78.4 us
    pallas_call x1, Pallas kernels: 84.7 us -> 78.4 us  [local(): pl.pallas_call(functools.partial(kernel, bands, slabs), out_shape=[jax.Sh...]
where the time goes in v3:
time: 79.9 us; the launch traced here: 79.8 us
  Pallas kernels  78.4 us (98%)
  other arithmetic  1.34 us (2%)
    pallas_call x1, Pallas kernels, local(): pl.pallas_call(functools.partial(kernel, bands, slabs), out_shape=[jax.Sh...  78.4 us

profile of v3, /device:TPU:6, one launch (start us, length us, event | category | flops | bytes accessed | tf_op | source)
XLA Modules:
  0.0 79.8 jit_solution(12694937335489735595)
XLA Ops:
  0.0 78.4 %exchange.1 = (f32[2,10,160,128]{3,2,1,0:T(8,128)S(1)}, f32[2,10,160,128]{3,2,1,0:T(8,128)S(1)}) custom-call(s32[2,2,32]{2,1,0:T(2,128)} %bitcast.1, f32[2,10,160,128]{3,2,1,0:T(8,128)} %orbitals.1, f32[128,128]{1,0:T(8,128)} %constant.6.clone.table_x_hbm, f32[160,160]{1,0:T(8,128)} %constant.7.clone.table_y_hbm, f32[5,160,128]{2,1,0:T(8,128)} %constant.8.clone.modes_hbm), custom_call_target="tpu_custom_call" | custom-call | tf_op jit(solution)/shard_map/exchange/pallas_call | solution.py:422
  78.4 1.3 %add.3 = f32[2,10,160,128]{3,2,1,0:T(8,128)} add(f32[2,10,160,128]{3,2,1,0:T(8,128)S(1)} %get-tuple-element.7, f32[2,10,160,128]{3,2,1,0:T(8,128)S(1)} %get-tuple-element.8) | non-fusion elementwise | flops 409600 | bytes 4915200 | tf_op jit(solution)/shard_map/add | solution.py:457

commit v4 on v3

--- a/solution.py
+++ b/solution.py
@@ -307,17 +307,17 @@
     def potential(c, a, z):
         return times_x(times_y(along_y[...], field[c, a, z]), along_x[...]) * weights[a][c]
 
-    def first_potential(g):
+    def first_potential(c, g):
         for step in range(GROUP):
             z = g * GROUP + step
-            field[0, 0, z] = potential(0, 0, z)
+            field[c, 0, z] = potential(c, 0, z)
 
     def inverse(c, g):
         for step in range(GROUP):
             z = g * GROUP + step
             total = None
             for a in range(band_dev):
-                value = field[0, 0, z] if a == c == 0 else potential(c, a, z)
+                value = field[c, 0, z] if a == 0 else potential(c, a, z)
                 term = value * own[a, z]
                 total = term if total is None else total + term
                 mutual = value * part[c, z]
@@ -359,11 +359,11 @@
     owner_wait(late)
     combine(late)
     summarise(1, 1)
-    settle(0, 0)
-    loop(0, groups, first_potential)
     resolve(late)
     send_back(late, 0)
     send_back(late, 1)
+    settle(0, 0)
+    loop(0, groups, functools.partial(first_potential, 0))
 
     @pl.when(core == 1)
     def _():
@@ -381,6 +381,7 @@
 
     loop(1, groups, functools.partial(inverse, 0))
     settle(0, 1)
+    loop(0, groups, functools.partial(first_potential, 1))
     settle(1, 1)
     loop(0, groups, functools.partial(inverse, 1))
 

time: 79.9 us -> 79 us (0.989)
  Pallas kernels: 78.4 us -> 77.5 us
    pallas_call x1, Pallas kernels: 78.4 us -> 77.5 us  [local(): pl.pallas_call(functools.partial(kernel, bands, slabs), out_shape=[jax.Sh...]
where the time goes in v4:
time: 79 us; the launch traced here: 78.8 us
  Pallas kernels  77.5 us (98%)
  other arithmetic  1.34 us (2%)
    pallas_call x1, Pallas kernels, local(): pl.pallas_call(functools.partial(kernel, bands, slabs), out_shape=[jax.Sh...  77.5 us

profile of v4, /device:TPU:6, one launch (start us, length us, event | category | flops | bytes accessed | tf_op | source)
XLA Modules:
  0.0 78.8 jit_solution(7578359386754011234)
XLA Ops:
  0.0 77.5 %exchange.1 = (f32[2,10,160,128]{3,2,1,0:T(8,128)S(1)}, f32[2,10,160,128]{3,2,1,0:T(8,128)S(1)}) custom-call(s32[2,2,32]{2,1,0:T(2,128)} %bitcast.1, f32[2,10,160,128]{3,2,1,0:T(8,128)} %orbitals.1, f32[128,128]{1,0:T(8,128)} %constant.6.clone.table_x_hbm, f32[160,160]{1,0:T(8,128)} %constant.7.clone.table_y_hbm, f32[5,160,128]{2,1,0:T(8,128)} %constant.8.clone.modes_hbm), custom_call_target="tpu_custom_call" | custom-call | tf_op jit(solution)/shard_map/exchange/pallas_call | solution.py:423
  77.5 1.3 %add.3 = f32[2,10,160,128]{3,2,1,0:T(8,128)} add(f32[2,10,160,128]{3,2,1,0:T(8,128)S(1)} %get-tuple-element.7, f32[2,10,160,128]{3,2,1,0:T(8,128)S(1)} %get-tuple-element.8) | non-fusion elementwise | flops 409600 | bytes 4915200 | tf_op jit(solution)/shard_map/add | solution.py:458

commit v5 on v4

--- a/solution.py
+++ b/solution.py
@@ -356,9 +356,9 @@
         send_back(0, 1)
         send_back(0, 0)
 
+    summarise(1, 1)
     owner_wait(late)
     combine(late)
-    summarise(1, 1)
     resolve(late)
     send_back(late, 0)
     send_back(late, 1)

time: 79 us -> 78.9 us (level)
  no operation moved by 1% of the time
where the time goes in v5:
time: 78.9 us; the launch traced here: 78.8 us
  Pallas kernels  77.5 us (98%)
  other arithmetic  1.34 us (2%)
    pallas_call x1, Pallas kernels, local(): pl.pallas_call(functools.partial(kernel, bands, slabs), out_shape=[jax.Sh...  77.5 us

profile of v5, /device:TPU:6, one launch (start us, length us, event | category | flops | bytes accessed | tf_op | source)
XLA Modules:
  0.0 78.8 jit_solution(10639625036458914802)
XLA Ops:
  0.0 77.5 %exchange.1 = (f32[2,10,160,128]{3,2,1,0:T(8,128)S(1)}, f32[2,10,160,128]{3,2,1,0:T(8,128)S(1)}) custom-call(s32[2,2,32]{2,1,0:T(2,128)} %bitcast.1, f32[2,10,160,128]{3,2,1,0:T(8,128)} %orbitals.1, f32[128,128]{1,0:T(8,128)} %constant.6.clone.table_x_hbm, f32[160,160]{1,0:T(8,128)} %constant.7.clone.table_y_hbm, f32[5,160,128]{2,1,0:T(8,128)} %constant.8.clone.modes_hbm), custom_call_target="tpu_custom_call" | custom-call | tf_op jit(solution)/shard_map/exchange/pallas_call | solution.py:423
  77.5 1.3 %add.3 = f32[2,10,160,128]{3,2,1,0:T(8,128)} add(f32[2,10,160,128]{3,2,1,0:T(8,128)S(1)} %get-tuple-element.7, f32[2,10,160,128]{3,2,1,0:T(8,128)S(1)} %get-tuple-element.8) | non-fusion elementwise | flops 409600 | bytes 4915200 | tf_op jit(solution)/shard_map/add | solution.py:458

commit v6 on v5

--- a/solution.py
+++ b/solution.py
@@ -83,7 +83,33 @@
     chips = members // CORES
     chunk = rows // chips
     groups = planes // GROUP
-
+    far_first = sorted(range(1, chips), key=lambda j: -min(j, chips - j))
+
+    band = lax.axis_index("band")
+    slab = lax.axis_index("slab")
+    core = lax.rem(slab, CORES)
+    half = slab // members
+    me = lax.rem(slab, members)
+    chip = me // CORES
+    lower = half == 0
+
+    ahead = lax.rem(band + 1, bands)
+    behind = lax.rem(band + bands - 1, bands)
+    partner = jnp.where(core == 0, ahead, behind)
+    giver = jnp.where(core == 0, behind, ahead)
+    partner_id = {"band": partner, "slab": slab}
+    giver_id = {"band": giver, "slab": slab}
+    across_id = {"band": band, "slab": lax.rem(slab + members, slabs)}
+
+    def member_id(member):
+        same = lax.rem(member, CORES) == core
+        return {"band": jnp.where(same, band, partner), "slab": half * members + member}
+
+    barrier = pltpu.get_barrier_semaphore()
+    everyone = [across_id, giver_id, partner_id]
+    everyone += [member_id(lax.rem(me + k, members)) for k in range(1, members)]
+    for device in everyone:
+        pl.semaphore_signal(barrier, inc=1, device_id=device, device_id_type=MESH)
     loads = [
         pltpu.make_async_copy(source, target, load.at[i])
         for i, (source, target) in enumerate(
@@ -99,31 +125,6 @@
     for copy in loads:
         copy.start()
 
-    band = lax.axis_index("band")
-    slab = lax.axis_index("slab")
-    core = lax.rem(slab, CORES)
-    half = slab // members
-    me = lax.rem(slab, members)
-    chip = me // CORES
-    lower = half == 0
-
-    ahead = lax.rem(band + 1, bands)
-    behind = lax.rem(band + bands - 1, bands)
-    partner = jnp.where(core == 0, ahead, behind)
-    giver = jnp.where(core == 0, behind, ahead)
-    partner_id = {"band": partner, "slab": slab}
-    giver_id = {"band": giver, "slab": slab}
-    across_id = {"band": band, "slab": lax.rem(slab + members, slabs)}
-
-    def member_id(member):
-        same = lax.rem(member, CORES) == core
-        return {"band": jnp.where(same, band, partner), "slab": half * members + member}
-
-    barrier = pltpu.get_barrier_semaphore()
-    everyone = [partner_id, giver_id, across_id]
-    everyone += [member_id(lax.rem(me + k, members)) for k in range(1, members)]
-    for device in everyone:
-        pl.semaphore_signal(barrier, inc=1, device_id=device, device_id_type=MESH)
     pl.semaphore_wait(barrier, len(everyone))
 
     def remote(source, target, send, recv, device):
@@ -237,7 +238,7 @@
             return 0
 
         lax.fori_loop(0, chips, body, 0)
-        for j in range(1, chips):
+        for j in far_first:
             owner_copy(a, c, j).start()
         slot, owner = pair(core, a, c)
         pl.when(core != owner)(lambda: owner_copy(a, c, 0).start())
@@ -281,7 +282,7 @@
         at_member[core, t, chip] = from_owner[t, me]
 
     def send_back(t, other_core):
-        for j in range(1 - other_core, chips):
+        for j in far_first + [0] * other_core:
             member_copy(t, other_core, j).start()
 
     def solve(c, a):

time: 78.9 us -> 78.7 us (level)
  no operation moved by 1% of the time
where the time goes in v6:
time: 78.7 us; the launch traced here: 78.6 us
  Pallas kernels  77.2 us (98%)
  other arithmetic  1.34 us (2%)
    pallas_call x1, Pallas kernels, local(): pl.pallas_call(functools.partial(kernel, bands, slabs), out_shape=[jax.Sh...  77.2 us

profile of v6, /device:TPU:6, one launch (start us, length us, event | category | flops | bytes accessed | tf_op | source)
XLA Modules:
  0.0 78.6 jit_solution(14943452668490487963)
XLA Ops:
  0.0 77.2 %exchange.1 = (f32[2,10,160,128]{3,2,1,0:T(8,128)S(1)}, f32[2,10,160,128]{3,2,1,0:T(8,128)S(1)}) custom-call(s32[2,2,32]{2,1,0:T(2,128)} %bitcast.1, f32[2,10,160,128]{3,2,1,0:T(8,128)} %orbitals.1, f32[128,128]{1,0:T(8,128)} %constant.6.clone.table_x_hbm, f32[160,160]{1,0:T(8,128)} %constant.7.clone.table_y_hbm, f32[5,160,128]{2,1,0:T(8,128)} %constant.8.clone.modes_hbm), custom_call_target="tpu_custom_call" | custom-call | tf_op jit(solution)/shard_map/exchange/pallas_call | solution.py:424
  77.2 1.3 %add.3 = f32[2,10,160,128]{3,2,1,0:T(8,128)} add(f32[2,10,160,128]{3,2,1,0:T(8,128)S(1)} %get-tuple-element.7, f32[2,10,160,128]{3,2,1,0:T(8,128)S(1)} %get-tuple-element.8) | non-fusion elementwise | flops 409600 | bytes 4915200 | tf_op jit(solution)/shard_map/add | solution.py:459
